TPU v7x, 256 devices: a whole 4x4x8 slice. The times are simulated.
256 devices in a mesh: seq: 64 (over z, y, core), rep: 4 (over x).
Axes of the slice: x: 4, y: 4, z: 8, core: 2. Of those that a mesh axis runs over, the one named last changes fastest.
Arguments:
- query_rows: bfloat16 [98304, 1024], P(('seq', 'rep')), may hold values from -6 to 6
- key_rows: bfloat16 [98304, 128], P(('seq', 'rep')), may hold values from -6 to 6
- value_rows: bfloat16 [98304, 128], P(('seq', 'rep')), may hold values from -6 to 6
- out_grad: bfloat16 [98304, 1024], P(('seq', 'rep')), may hold values from -1.5 to 1.5
- logsumexp: float32 [8, 98304], P(None, ('seq', 'rep')), may hold values from 1 to 3
- row_delta: float32 [8, 98304], P(None, ('seq', 'rep')), may hold values from -8 to 8
- doc_lengths: int32 [255], replicated, may hold values from 1 to 1537, as said below
Outputs:
- query_grad: bfloat16 [98304, 1024], P(('seq', 'rep'))
- key_grad: bfloat16 [98304, 128], P(('seq', 'rep'))
- value_grad: bfloat16 [98304, 128], P(('seq', 'rep'))
Inputs may be any that keep to these rules, and one draw needn't show every extreme that they name: `doc_lengths`: 255 document lengths in pack order, summing to 98304; so every document lies within 5 consecutive aligned blocks of 384 positions.
All inputs are finite; a program needn't handle non-finite values.
Results may differ from a plain program's by a relative error of at most 0.019.
Values may be sent and summed in bfloat16 or wider, within the bound.
No kernel may reach another device: no remote copies, remote signals or barrier semaphores. Data moves between devices by JAX's collectives and lax.ppermute only.
A program may use at most 64 MiB of HBM per device.

v0:
```python
import jax
import jax.numpy as jnp
from jax import lax
from jax.sharding import PartitionSpec as P

REACH = 4


def from_behind(array, axis, by):
    length = lax.axis_size(axis)
    pairs = [(i, i + by) for i in range(length) if 0 <= i + by < length]
    return lax.ppermute(array, axis, pairs)


def doc_index(positions, doc_ends):
    return jnp.sum((doc_ends[None, :] <= positions[:, None]).astype(jnp.int32), axis=1)


def block_grads(
    query_block,
    grad_block,
    stat_block,
    delta_block,
    key_block,
    value_block,
    query_docs,
    key_docs,
    query_pos,
    key_pos,
):
    row_count = query_block.shape[0]
    head_size = key_block.shape[1]
    head_count = query_block.shape[1] // head_size
    score_scale = head_size ** (-0.5)
    query_heads = query_block.reshape(row_count, head_count, head_size)
    grad_heads = grad_block.reshape(row_count, head_count, head_size)
    scores = (
        jnp.einsum("qhd,kd->hqk", query_heads, key_block, preferred_element_type=jnp.float32)
        * score_scale
    )
    allowed = (query_docs[:, None] == key_docs[None, :]) & (key_pos[None, :] <= query_pos[:, None])
    probs = jnp.where(allowed[None], jnp.exp(scores - stat_block[:, :, None]), 0.0)
    dprobs = jnp.einsum("qhd,kd->hqk", grad_heads, value_block, preferred_element_type=jnp.float32)
    dscores = probs * (dprobs - delta_block[:, :, None])
    dscores_half = dscores.astype(jnp.bfloat16)
    query_part = (
        jnp.einsum("hqk,kd->qhd", dscores_half, key_block, preferred_element_type=jnp.float32)
        * score_scale
    ).reshape(row_count, head_count * head_size)
    probs_half = probs.astype(jnp.bfloat16)
    key_part = (
        jnp.einsum("hqk,qhd->kd", dscores_half, query_heads, preferred_element_type=jnp.float32)
        * score_scale
    )
    value_part = jnp.einsum(
        "hqk,qhd->kd", probs_half, grad_heads, preferred_element_type=jnp.float32
    )
    return (query_part, key_part, value_part)


def shards(query_rows, key_rows, value_rows, out_grad, logsumexp, row_delta, doc_lengths):
    shard_rows = query_rows.shape[0]
    first_row = lax.axis_index(("seq", "rep")) * shard_rows
    doc_ends = jnp.cumsum(doc_lengths)
    own_pos = first_row + jnp.arange(shard_rows, dtype=jnp.int32)
    own_docs = doc_index(own_pos, doc_ends)
    query_total, key_total, value_total = block_grads(
        query_rows,
        out_grad,
        logsumexp,
        row_delta,
        key_rows,
        value_rows,
        own_docs,
        own_docs,
        own_pos,
        own_pos,
    )
    for distance in range(1, REACH + 1):
        prev_pos = own_pos - distance * shard_rows
        prev_docs = jnp.where(prev_pos >= 0, doc_index(prev_pos, doc_ends), -1)
        prev_key, prev_value = from_behind((key_rows, value_rows), ("seq", "rep"), distance)
        cross_q, cross_k, cross_v = block_grads(
            query_rows,
            out_grad,
            logsumexp,
            row_delta,
            prev_key,
            prev_value,
            own_docs,
            prev_docs,
            own_pos,
            prev_pos,
        )
        extra_k, extra_v = (
            from_behind(cross_k.astype(jnp.bfloat16), ("seq", "rep"), -distance).astype(
                cross_k.dtype
            ),
            from_behind(cross_v.astype(jnp.bfloat16), ("seq", "rep"), -distance).astype(
                cross_v.dtype
            ),
        )
        query_total = query_total + cross_q
        key_total = key_total + extra_k
        value_total = value_total + extra_v
    return (
        query_total.astype(jnp.bfloat16),
        key_total.astype(jnp.bfloat16),
        value_total.astype(jnp.bfloat16),
    )


def solution(mesh):
    return jax.shard_map(
        shards,
        mesh=mesh,
        in_specs=(
            P(("seq", "rep"), None),
            P(("seq", "rep"), None),
            P(("seq", "rep"), None),
            P(("seq", "rep"), None),
            P(None, ("seq", "rep")),
            P(None, ("seq", "rep")),
            P(),
        ),
        out_specs=(P(("seq", "rep"), None), P(("seq", "rep"), None), P(("seq", "rep"), None)),
        check_vma=False,
    )
```

profile of v0, /device:TPU:145, one launch (start us, length us, event | category | flops | bytes accessed | tf_op | source)
XLA Modules:
  0.0 99.8 jit_solution(2680649066163441781)
XLA Ops:
  0.7 4.8 %collective-permute-start.3 = (bf16[384,128]{1,0:T(8,128)(2,1)}, bf16[384,128]{1,0:T(8,128)(2,1)S(1)}, u32[]{:S(2)}, u32[]{:S(2)}) collective-permute-start(bf16[384,128]{1,0:T(8,128)(2,1)} %param.9), channel_id=1, source_target_pairs={{0,2},{1,3},{2,4},{3,5},{4,6},{5,7},{6,8},{7,9},{8,10},{9,11},{10,... | collective-permute-start | bytes 294920 | tf_op jit(solution)/shard_map/ppermute | solution.py:12
  5.5 2.2 %collective-permute-start.1 = (bf16[384,128]{1,0:T(8,128)(2,1)}, bf16[384,128]{1,0:T(8,128)(2,1)S(1)}, u32[]{:S(2)}, u32[]{:S(2)}) collective-permute-start(bf16[384,128]{1,0:T(8,128)(2,1)} %param.9), channel_id=1, source_target_pairs={{0,1},{1,2},{2,3},{3,4},{4,5},{5,6},{6,7},{7,8},{8,9},{9,10},{10,1... | collective-permute-start | bytes 294920 | tf_op jit(solution)/shard_map/ppermute | solution.py:12
  7.7 4.0 %collective-permute-start.7 = (bf16[384,128]{1,0:T(8,128)(2,1)}, bf16[384,128]{1,0:T(8,128)(2,1)S(1)}, u32[]{:S(2)}, u32[]{:S(2)}) collective-permute-start(bf16[384,128]{1,0:T(8,128)(2,1)} %param.9), channel_id=1, source_target_pairs={{0,4},{1,5},{2,6},{3,7},{4,8},{5,9},{6,10},{7,11},{8,12},{9,13},{1... | collective-permute-start | bytes 294920 | tf_op jit(solution)/shard_map/ppermute | solution.py:12
  11.7 3.7 %collective-permute-start.5 = (bf16[384,128]{1,0:T(8,128)(2,1)}, bf16[384,128]{1,0:T(8,128)(2,1)S(1)}, u32[]{:S(2)}, u32[]{:S(2)}) collective-permute-start(bf16[384,128]{1,0:T(8,128)(2,1)} %param.9), channel_id=1, source_target_pairs={{0,3},{1,4},{2,5},{3,6},{4,7},{5,8},{6,9},{7,10},{8,11},{9,12},{10... | collective-permute-start | bytes 294920 | tf_op jit(solution)/shard_map/ppermute | solution.py:12
  15.5 1.9 %collective-permute-start.4 = (bf16[384,128]{1,0:T(8,128)(2,1)}, bf16[384,128]{1,0:T(8,128)(2,1)S(1)}, u32[]{:S(2)}, u32[]{:S(2)}) collective-permute-start(bf16[384,128]{1,0:T(8,128)(2,1)} %param.8), channel_id=1, source_target_pairs={{0,3},{1,4},{2,5},{3,6},{4,7},{5,8},{6,9},{7,10},{8,11},{9,12},{10... | collective-permute-start | bytes 294920 | tf_op jit(solution)/shard_map/ppermute | solution.py:12
  19.4 2.0 %fusion.99 = f32[384,384,8]{1,0,2:T(8,128)S(1)} fusion(bf16[384,128]{1,0:T(8,128)(2,1)} %param.8, bf16[384,1024]{1,0:T(8,128)(2,1)} %param.7), kind=kOutput, calls=%fused_computation.92 | convolution fusion | flops 301989888 | bytes 5603328 | tf_op jit(solution)/shard_map/qhd,kd->hqk/dot_general | solution.py:38
  22.3 1.2 %copy-done.2 = f32[384,384,8]{1,0,2:T(8,128)} copy-done((f32[384,384,8]{1,0,2:T(8,128)}, f32[384,384,8]{1,0,2:T(8,128)S(1)}, u32[]{:S(2)}) %copy-start.2) | copy-done | bytes 4718616
  23.6 1.7 %fusion.17 = bf16[8,384,384]{1,2,0:T(8,128)(2,1)S(1)} fusion(f32[384,384,8]{1,0,2:T(8,128)S(1)} %fusion.99, f32[8,384]{1,0:T(8,128)S(1)} %copy-done.7, f32[8,384]{1,0:T(8,128)S(1)} %copy-done.8, pred[384,384]{0,1:T(8,128)(4,1)S(1)} %get-tuple-element.20, bf16[384,128]{1,0:T(8,128)(2,1)S(1)} %copy-done.6, bf16[384,1024]{1,0:T(8,128)(2,1)S(1)} %copy-done), kind=kOutput, calls=%fused_computation.26 | convolution fusion | flops 309067776 | bytes 8134656 | tf_op jit(solution)/shard_map/qhd,kd->hqk/dot_general | solution.py:43
  26.7 3.0 %collective-permute-start.6 = (bf16[384,128]{1,0:T(8,128)(2,1)S(1)}, bf16[384,128]{1,0:T(8,128)(2,1)S(1)}, u32[]{:S(2)}, u32[]{:S(2)}) collective-permute-start(bf16[384,128]{1,0:T(8,128)(2,1)S(1)} %copy-done.5), channel_id=1, source_target_pairs={{0,4},{1,5},{2,6},{3,7},{4,8},{5,9},{6,10},{7,11},{8,12},{9,13},{1... | collective-permute-start | bytes 294920 | tf_op jit(solution)/shard_map/ppermute | solution.py:12
  30.5 1.0 fusion.63
  31.5 3.1 %collective-permute-start = (bf16[384,128]{1,0:T(8,128)(2,1)S(1)}, bf16[384,128]{1,0:T(8,128)(2,1)S(1)}, u32[]{:S(2)}, u32[]{:S(2)}) collective-permute-start(bf16[384,128]{1,0:T(8,128)(2,1)S(1)} %copy-done.5), channel_id=1, source_target_pairs={{0,1},{1,2},{2,3},{3,4},{4,5},{5,6},{6,7},{7,8},{8,9},{9,10},{10,1... | collective-permute-start | bytes 294920 | tf_op jit(solution)/shard_map/ppermute | solution.py:12
  35.4 1.0 fusion.60
  36.4 1.9 %collective-permute-start.2 = (bf16[384,128]{1,0:T(8,128)(2,1)S(1)}, bf16[384,128]{1,0:T(8,128)(2,1)S(1)}, u32[]{:S(2)}, u32[]{:S(2)}) collective-permute-start(bf16[384,128]{1,0:T(8,128)(2,1)S(1)} %copy-done.5), channel_id=1, source_target_pairs={{0,2},{1,3},{2,4},{3,5},{4,6},{5,7},{6,8},{7,9},{8,10},{9,11},{10,... | collective-permute-start | bytes 294920 | tf_op jit(solution)/shard_map/ppermute | solution.py:12
  38.3 1.7 %fusion.5 = bf16[8,384,384]{1,2,0:T(8,128)(2,1)S(1)} fusion(f32[384,384,8]{1,0,2:T(8,128)S(1)} %fusion.93, f32[8,384]{1,0:T(8,128)S(1)} %copy-done.7, f32[8,384]{1,0:T(8,128)S(1)} %copy-done.8, pred[384,384]{0,1:T(8,128)(4,1)S(1)} %get-tuple-element.18, bf16[384,128]{1,0:T(8,128)(2,1)S(1)} %collective-permute-done.5, bf16[384,1024]{1,0:T(8,128)(2,1)S(1)} %copy-done), kind=kOutput, calls=%fused_computation.8 | convolution fusion | flops 309067776 | bytes 8134656 | tf_op jit(solution)/shard_map/qhd,kd->hqk/dot_general | solution.py:43
  40.8 3.0 %collective-permute-done.2 = bf16[384,128]{1,0:T(8,128)(2,1)S(1)} collective-permute-done((bf16[384,128]{1,0:T(8,128)(2,1)S(1)}, bf16[384,128]{1,0:T(8,128)(2,1)S(1)}, u32[]{:S(2)}, u32[]{:S(2)}) %collective-permute-start.2) | collective-permute-done | bytes 98336 | tf_op jit(solution)/shard_map/ppermute | solution.py:12
  43.8 4.6 %collective-permute-start.10 = (bf16[384,128]{1,0:T(8,128)(2,1)S(1)}, bf16[384,128]{1,0:T(8,128)(2,1)S(1)}, u32[]{:S(2)}, u32[]{:S(2)}) collective-permute-start(bf16[384,128]{1,0:T(8,128)(2,1)S(1)} %fusion.73), channel_id=1, source_target_pairs={{3,0},{4,1},{5,2},{6,3},{7,4},{8,5},{9,6},{10,7},{11,8},{12,9},{13... | collective-permute-start | bytes 294920 | tf_op jit(solution)/shard_map/ppermute | solution.py:12
  49.2 1.0 fusion.66
  50.2 2.3 %collective-permute-start.14 = (bf16[384,128]{1,0:T(8,128)(2,1)S(1)}, bf16[384,128]{1,0:T(8,128)(2,1)S(1)}, u32[]{:S(2)}, u32[]{:S(2)}) collective-permute-start(bf16[384,128]{1,0:T(8,128)(2,1)S(1)} %fusion.63), channel_id=1, source_target_pairs={{3,0},{4,1},{5,2},{6,3},{7,4},{8,5},{9,6},{10,7},{11,8},{12,9},{13... | collective-permute-start | bytes 294920 | tf_op jit(solution)/shard_map/ppermute | solution.py:12
  52.5 1.7 %fusion.1 = bf16[8,384,384]{1,2,0:T(8,128)(2,1)S(1)} fusion(f32[384,384,8]{1,0,2:T(8,128)S(1)} %fusion.91, f32[8,384]{1,0:T(8,128)S(1)} %copy-done.7, f32[8,384]{1,0:T(8,128)S(1)} %copy-done.8, pred[384,384]{0,1:T(8,128)(4,1)S(1)} %get-tuple-element.17, bf16[384,128]{1,0:T(8,128)(2,1)S(1)} %collective-permute-done.7, bf16[384,1024]{1,0:T(8,128)(2,1)S(1)} %copy-done), kind=kOutput, calls=%fused_computation.2 | convolution fusion | flops 309067776 | bytes 8134656 | tf_op jit(solution)/shard_map/qhd,kd->hqk/dot_general | solution.py:43
  55.0 2.1 %collective-permute-start.15 = (bf16[384,128]{1,0:T(8,128)(2,1)S(1)}, bf16[384,128]{1,0:T(8,128)(2,1)S(1)}, u32[]{:S(2)}, u32[]{:S(2)}) collective-permute-start(bf16[384,128]{1,0:T(8,128)(2,1)S(1)} %fusion.60), channel_id=1, source_target_pairs={{4,0},{5,1},{6,2},{7,3},{8,4},{9,5},{10,6},{11,7},{12,8},{13,9},{1... | collective-permute-start | bytes 294920 | tf_op jit(solution)/shard_map/ppermute | solution.py:12
  57.1 1.7 %fusion.9 = bf16[8,384,384]{1,2,0:T(8,128)(2,1)S(1)} fusion(f32[384,384,8]{1,0,2:T(8,128)S(1)} %fusion.95, f32[8,384]{1,0:T(8,128)S(1)} %copy-done.7, f32[8,384]{1,0:T(8,128)S(1)} %copy-done.8, pred[384,384]{0,1:T(8,128)(4,1)S(1)} %get-tuple-element.19, bf16[384,128]{1,0:T(8,128)(2,1)S(1)} %collective-permute-done.3, bf16[384,1024]{1,0:T(8,128)(2,1)S(1)} %copy-done), kind=kOutput, calls=%fused_computation.14 | convolution fusion | flops 309067776 | bytes 8134656 | tf_op jit(solution)/shard_map/qhd,kd->hqk/dot_general | solution.py:43
  59.7 7.4 %collective-permute-start.13 = (bf16[384,128]{1,0:T(8,128)(2,1)S(1)}, bf16[384,128]{1,0:T(8,128)(2,1)}, u32[]{:S(2)}, u32[]{:S(2)}) collective-permute-start(bf16[384,128]{1,0:T(8,128)(2,1)S(1)} %fusion.66), channel_id=1, source_target_pairs={{2,0},{3,1},{4,2},{5,3},{6,4},{7,5},{8,6},{9,7},{10,8},{11,9},{12,... | collective-permute-start | bytes 294920 | tf_op jit(solution)/shard_map/ppermute | solution.py:12
  67.8 1.6 %fusion.69 = bf16[384,128]{1,0:T(8,128)(2,1)} fusion(f32[384,384,8]{1,0,2:T(8,128)S(1)} %fusion.97, f32[8,384]{1,0:T(8,128)S(1)} %copy-done.8, pred[384,384]{0,1:T(8,128)(4,1)S(1)} %get-tuple-element.21, bf16[384,1024]{1,0:T(8,128)(2,1)S(1)} %copy-done), kind=kOutput, calls=%fused_computation.64 | convolution fusion | flops 306757632 | bytes 5763072 | tf_op jit(solution)/shard_map/hqk,qhd->kd/dot_general | solution.py:55
  69.5 1.7 %fusion.13 = bf16[8,384,384]{1,2,0:T(8,128)(2,1)S(1)} fusion(f32[384,384,8]{1,0,2:T(8,128)S(1)} %fusion.97, f32[8,384]{1,0:T(8,128)S(1)} %copy-done.7, f32[8,384]{1,0:T(8,128)S(1)} %copy-done.8, pred[384,384]{0,1:T(8,128)(4,1)S(1)} %get-tuple-element.21, bf16[384,128]{1,0:T(8,128)(2,1)S(1)} %collective-permute-done.1, bf16[384,1024]{1,0:T(8,128)(2,1)S(1)} %copy-done), kind=kOutput, calls=%fused_computation.20 | convolution fusion | flops 309067776 | bytes 8134656 | tf_op jit(solution)/shard_map/qhd,kd->hqk/dot_general | solution.py:43
  72.0 2.3 %collective-permute-start.12 = (bf16[384,128]{1,0:T(8,128)(2,1)}, bf16[384,128]{1,0:T(8,128)(2,1)}, u32[]{:S(2)}, u32[]{:S(2)}) collective-permute-start(bf16[384,128]{1,0:T(8,128)(2,1)} %fusion.69), channel_id=1, source_target_pairs={{1,0},{2,1},{3,2},{4,3},{5,4},{6,5},{7,6},{8,7},{9,8},{10,9},{11,1... | collective-permute-start | bytes 294920 | tf_op jit(solution)/shard_map/ppermute | solution.py:12
  76.2 0.9 multiply_convert_fusion
  77.1 1.2 %copy.102 = bf16[384,1024]{1,0:T(8,128)(2,1)} copy(bf16[384,1024]{0,1:T(8,128)(2,1)S(1)} %bitcast.328) | data formatting | bytes 1572864
  78.3 2.5 %collective-permute-start.11 = (bf16[384,128]{1,0:T(8,128)(2,1)S(1)}, bf16[384,128]{1,0:T(8,128)(2,1)S(1)}, u32[]{:S(2)}, u32[]{:S(2)}) collective-permute-start(bf16[384,128]{1,0:T(8,128)(2,1)S(1)} %fusion.72), channel_id=1, source_target_pairs={{4,0},{5,1},{6,2},{7,3},{8,4},{9,5},{10,6},{11,7},{12,8},{13,9},{1... | collective-permute-start | bytes 294920 | tf_op jit(solution)/shard_map/ppermute | solution.py:12
  80.8 8.1 %collective-permute-start.9 = (bf16[384,128]{1,0:T(8,128)(2,1)S(1)}, bf16[384,128]{1,0:T(8,128)(2,1)S(1)}, u32[]{:S(2)}, u32[]{:S(2)}) collective-permute-start(bf16[384,128]{1,0:T(8,128)(2,1)S(1)} %fusion.74), channel_id=1, source_target_pairs={{2,0},{3,1},{4,2},{5,3},{6,4},{7,5},{8,6},{9,7},{10,8},{11,9},{12,... | collective-permute-start | bytes 294920 | tf_op jit(solution)/shard_map/ppermute | solution.py:12
  88.8 5.4 %collective-permute-start.8 = (bf16[384,128]{1,0:T(8,128)(2,1)S(1)}, bf16[384,128]{1,0:T(8,128)(2,1)S(1)}, u32[]{:S(2)}, u32[]{:S(2)}) collective-permute-start(bf16[384,128]{1,0:T(8,128)(2,1)S(1)} %fusion.75), channel_id=1, source_target_pairs={{1,0},{2,1},{3,2},{4,3},{5,4},{6,5},{7,6},{8,7},{9,8},{10,9},{11,1... | collective-permute-start | bytes 294920 | tf_op jit(solution)/shard_map/ppermute | solution.py:12
  94.3 4.1 %add_convert_fusion = bf16[384,128]{1,0:T(8,128)(2,1)} fusion(bf16[384,128]{1,0:T(8,128)(2,1)S(1)} %collective-permute-done.15, bf16[384,128]{1,0:T(8,128)(2,1)S(1)} %collective-permute-done.14, bf16[384,128]{1,0:T(8,128)(2,1)} %collective-permute-done.13, bf16[384,128]{1,0:T(8,128)(2,1)} %collective-permute-done.12, f32[384,384,8]{1,0,2:T(8,128)} %copy-done.2, ...), kind=kOutput, calls=%fused_computation.104 | convolution fusion | flops 307150848 | bytes 6156288 | tf_op jit(solution)/shard_map/hqk,qhd->kd/dot_general | solution.py:55
  98.4 1.4 %add_convert_fusion.1 = bf16[384,128]{1,0:T(8,128)(2,1)} fusion(bf16[384,128]{1,0:T(8,128)(2,1)S(1)} %collective-permute-done.11, bf16[384,128]{1,0:T(8,128)(2,1)S(1)} %collective-permute-done.10, bf16[384,128]{1,0:T(8,128)(2,1)S(1)} %collective-permute-done.9, bf16[384,128]{1,0:T(8,128)(2,1)S(1)} %collective-permute-done.8, ...), kind=kOutput, calls=%fused_computation.105 | convolution fusion | flops 302481408 | bytes 3637248 | tf_op jit(solution)/shard_map/hqk,qhd->kd/dot_general | solution.py:52
  (59 shorter events, 12.4 us)
Async XLA Ops:
  0.6 22.9 %copy-start = (bf16[384,1024]{1,0:T(8,128)(2,1)S(1)}, bf16[384,1024]{1,0:T(8,128)(2,1)}, u32[]{:S(2)}) copy-start(bf16[384,1024]{1,0:T(8,128)(2,1)} %param.10) | copy-start | bytes 2359300
  0.6 22.9 %copy-start.6 = (bf16[384,128]{1,0:T(8,128)(2,1)S(1)}, bf16[384,128]{1,0:T(8,128)(2,1)}, u32[]{:S(2)}) copy-start(bf16[384,128]{1,0:T(8,128)(2,1)} %param.9) | copy-start | bytes 294916
  0.7 22.9 %copy-start.8 = (f32[8,384]{1,0:T(8,128)S(1)}, f32[8,384]{1,0:T(8,128)}, u32[]{:S(2)}) copy-start(f32[8,384]{1,0:T(8,128)} %param.11) | copy-start | bytes 36868
  0.7 22.9 %copy-start.7 = (f32[8,384]{1,0:T(8,128)S(1)}, f32[8,384]{1,0:T(8,128)}, u32[]{:S(2)}) copy-start(f32[8,384]{1,0:T(8,128)} %param.12) | copy-start | bytes 36868
  0.7 54.3 %collective-permute-start.3 = (bf16[384,128]{1,0:T(8,128)(2,1)}, bf16[384,128]{1,0:T(8,128)(2,1)S(1)}, u32[]{:S(2)}, u32[]{:S(2)}) collective-permute-start(bf16[384,128]{1,0:T(8,128)(2,1)} %param.9), channel_id=1, source_target_pairs={{0,2},{1,3},{2,4},{3,5},{4,6},{5,7},{6,8},{7,9},{8,10},{9,11},{10,... | collective-permute-start | bytes 294920 | tf_op jit(solution)/shard_map/ppermute | solution.py:12
  5.5 64.0 %collective-permute-start.1 = (bf16[384,128]{1,0:T(8,128)(2,1)}, bf16[384,128]{1,0:T(8,128)(2,1)S(1)}, u32[]{:S(2)}, u32[]{:S(2)}) collective-permute-start(bf16[384,128]{1,0:T(8,128)(2,1)} %param.9), channel_id=1, source_target_pairs={{0,1},{1,2},{2,3},{3,4},{4,5},{5,6},{6,7},{7,8},{8,9},{9,10},{10,1... | collective-permute-start | bytes 294920 | tf_op jit(solution)/shard_map/ppermute | solution.py:12
  7.7 42.5 %collective-permute-start.7 = (bf16[384,128]{1,0:T(8,128)(2,1)}, bf16[384,128]{1,0:T(8,128)(2,1)S(1)}, u32[]{:S(2)}, u32[]{:S(2)}) collective-permute-start(bf16[384,128]{1,0:T(8,128)(2,1)} %param.9), channel_id=1, source_target_pairs={{0,4},{1,5},{2,6},{3,7},{4,8},{5,9},{6,10},{7,11},{8,12},{9,13},{1... | collective-permute-start | bytes 294920 | tf_op jit(solution)/shard_map/ppermute | solution.py:12
  11.7 24.6 %collective-permute-start.5 = (bf16[384,128]{1,0:T(8,128)(2,1)}, bf16[384,128]{1,0:T(8,128)(2,1)S(1)}, u32[]{:S(2)}, u32[]{:S(2)}) collective-permute-start(bf16[384,128]{1,0:T(8,128)(2,1)} %param.9), channel_id=1, source_target_pairs={{0,3},{1,4},{2,5},{3,6},{4,7},{5,8},{6,9},{7,10},{8,11},{9,12},{10... | collective-permute-start | bytes 294920 | tf_op jit(solution)/shard_map/ppermute | solution.py:12
  15.5 10.5 %collective-permute-start.4 = (bf16[384,128]{1,0:T(8,128)(2,1)}, bf16[384,128]{1,0:T(8,128)(2,1)S(1)}, u32[]{:S(2)}, u32[]{:S(2)}) collective-permute-start(bf16[384,128]{1,0:T(8,128)(2,1)} %param.8), channel_id=1, source_target_pairs={{0,3},{1,4},{2,5},{3,6},{4,7},{5,8},{6,9},{7,10},{8,11},{9,12},{10... | collective-permute-start | bytes 294920 | tf_op jit(solution)/shard_map/ppermute | solution.py:12
  21.4 2.1 %copy-start.2 = (f32[384,384,8]{1,0,2:T(8,128)}, f32[384,384,8]{1,0,2:T(8,128)S(1)}, u32[]{:S(2)}) copy-start(f32[384,384,8]{1,0,2:T(8,128)S(1)} %fusion.99) | copy-start | bytes 14155780
  23.5 1.7 %copy-start.5 = (bf16[384,128]{1,0:T(8,128)(2,1)S(1)}, bf16[384,128]{1,0:T(8,128)(2,1)}, u32[]{:S(2)}) copy-start(bf16[384,128]{1,0:T(8,128)(2,1)} %param.8) | copy-start | bytes 294916
  23.5 6.1 %copy-start.1 = (bf16[384,1024]{1,0:T(8,128)(2,1)S(1)}, bf16[384,1024]{1,0:T(8,128)(2,1)}, u32[]{:S(2)}) copy-start(bf16[384,1024]{1,0:T(8,128)(2,1)} %param.7) | copy-start | bytes 2359300
  25.3 1.4 %copy-start.3 = (bf16[8,384,384]{1,2,0:T(8,128)(2,1)}, bf16[8,384,384]{1,2,0:T(8,128)(2,1)S(1)}, u32[]{:S(2)}) copy-start(bf16[8,384,384]{1,2,0:T(8,128)(2,1)S(1)} %fusion.17) | copy-start | bytes 7077892
  26.7 4.8 %collective-permute-start.6 = (bf16[384,128]{1,0:T(8,128)(2,1)S(1)}, bf16[384,128]{1,0:T(8,128)(2,1)S(1)}, u32[]{:S(2)}, u32[]{:S(2)}) collective-permute-start(bf16[384,128]{1,0:T(8,128)(2,1)S(1)} %copy-done.5), channel_id=1, source_target_pairs={{0,4},{1,5},{2,6},{3,7},{4,8},{5,9},{6,10},{7,11},{8,12},{9,13},{1... | collective-permute-start | bytes 294920 | tf_op jit(solution)/shard_map/ppermute | solution.py:12
  31.5 28.2 %collective-permute-start = (bf16[384,128]{1,0:T(8,128)(2,1)S(1)}, bf16[384,128]{1,0:T(8,128)(2,1)S(1)}, u32[]{:S(2)}, u32[]{:S(2)}) collective-permute-start(bf16[384,128]{1,0:T(8,128)(2,1)S(1)} %copy-done.5), channel_id=1, source_target_pairs={{0,1},{1,2},{2,3},{3,4},{4,5},{5,6},{6,7},{7,8},{8,9},{9,10},{10,1... | collective-permute-start | bytes 294920 | tf_op jit(solution)/shard_map/ppermute | solution.py:12
  36.4 7.4 %collective-permute-start.2 = (bf16[384,128]{1,0:T(8,128)(2,1)S(1)}, bf16[384,128]{1,0:T(8,128)(2,1)S(1)}, u32[]{:S(2)}, u32[]{:S(2)}) collective-permute-start(bf16[384,128]{1,0:T(8,128)(2,1)S(1)} %copy-done.5), channel_id=1, source_target_pairs={{0,2},{1,3},{2,4},{3,5},{4,6},{5,7},{6,8},{7,9},{8,10},{9,11},{10,... | collective-permute-start | bytes 294920 | tf_op jit(solution)/shard_map/ppermute | solution.py:12
  43.8 54.6 %collective-permute-start.10 = (bf16[384,128]{1,0:T(8,128)(2,1)S(1)}, bf16[384,128]{1,0:T(8,128)(2,1)S(1)}, u32[]{:S(2)}, u32[]{:S(2)}) collective-permute-start(bf16[384,128]{1,0:T(8,128)(2,1)S(1)} %fusion.73), channel_id=1, source_target_pairs={{3,0},{4,1},{5,2},{6,3},{7,4},{8,5},{9,6},{10,7},{11,8},{12,9},{13... | collective-permute-start | bytes 294920 | tf_op jit(solution)/shard_map/ppermute | solution.py:12
  50.2 28.1 %collective-permute-start.14 = (bf16[384,128]{1,0:T(8,128)(2,1)S(1)}, bf16[384,128]{1,0:T(8,128)(2,1)S(1)}, u32[]{:S(2)}, u32[]{:S(2)}) collective-permute-start(bf16[384,128]{1,0:T(8,128)(2,1)S(1)} %fusion.63), channel_id=1, source_target_pairs={{3,0},{4,1},{5,2},{6,3},{7,4},{8,5},{9,6},{10,7},{11,8},{12,9},{13... | collective-permute-start | bytes 294920 | tf_op jit(solution)/shard_map/ppermute | solution.py:12
  55.0 25.7 %collective-permute-start.15 = (bf16[384,128]{1,0:T(8,128)(2,1)S(1)}, bf16[384,128]{1,0:T(8,128)(2,1)S(1)}, u32[]{:S(2)}, u32[]{:S(2)}) collective-permute-start(bf16[384,128]{1,0:T(8,128)(2,1)S(1)} %fusion.60), channel_id=1, source_target_pairs={{4,0},{5,1},{6,2},{7,3},{8,4},{9,5},{10,6},{11,7},{12,8},{13,9},{1... | collective-permute-start | bytes 294920 | tf_op jit(solution)/shard_map/ppermute | solution.py:12
  59.7 29.2 %collective-permute-start.13 = (bf16[384,128]{1,0:T(8,128)(2,1)S(1)}, bf16[384,128]{1,0:T(8,128)(2,1)}, u32[]{:S(2)}, u32[]{:S(2)}) collective-permute-start(bf16[384,128]{1,0:T(8,128)(2,1)S(1)} %fusion.66), channel_id=1, source_target_pairs={{2,0},{3,1},{4,2},{5,3},{6,4},{7,5},{8,6},{9,7},{10,8},{11,9},{12,... | collective-permute-start | bytes 294920 | tf_op jit(solution)/shard_map/ppermute | solution.py:12
  72.0 22.3 %collective-permute-start.12 = (bf16[384,128]{1,0:T(8,128)(2,1)}, bf16[384,128]{1,0:T(8,128)(2,1)}, u32[]{:S(2)}, u32[]{:S(2)}) collective-permute-start(bf16[384,128]{1,0:T(8,128)(2,1)} %fusion.69), channel_id=1, source_target_pairs={{1,0},{2,1},{3,2},{4,3},{5,4},{6,5},{7,6},{8,7},{9,8},{10,9},{11,1... | collective-permute-start | bytes 294920 | tf_op jit(solution)/shard_map/ppermute | solution.py:12
  78.3 20.1 %copy-start.4 = (bf16[8,384,384]{1,2,0:T(8,128)(2,1)S(1)}, bf16[8,384,384]{1,2,0:T(8,128)(2,1)}, u32[]{:S(2)}) copy-start(bf16[8,384,384]{1,2,0:T(8,128)(2,1)} %copy-done.3) | copy-start | bytes 7077892
  78.3 20.0 %collective-permute-start.11 = (bf16[384,128]{1,0:T(8,128)(2,1)S(1)}, bf16[384,128]{1,0:T(8,128)(2,1)S(1)}, u32[]{:S(2)}, u32[]{:S(2)}) collective-permute-start(bf16[384,128]{1,0:T(8,128)(2,1)S(1)} %fusion.72), channel_id=1, source_target_pairs={{4,0},{5,1},{6,2},{7,3},{8,4},{9,5},{10,6},{11,7},{12,8},{13,9},{1... | collective-permute-start | bytes 294920 | tf_op jit(solution)/shard_map/ppermute | solution.py:12
  80.8 17.6 %collective-permute-start.9 = (bf16[384,128]{1,0:T(8,128)(2,1)S(1)}, bf16[384,128]{1,0:T(8,128)(2,1)S(1)}, u32[]{:S(2)}, u32[]{:S(2)}) collective-permute-start(bf16[384,128]{1,0:T(8,128)(2,1)S(1)} %fusion.74), channel_id=1, source_target_pairs={{2,0},{3,1},{4,2},{5,3},{6,4},{7,5},{8,6},{9,7},{10,8},{11,9},{12,... | collective-permute-start | bytes 294920 | tf_op jit(solution)/shard_map/ppermute | solution.py:12
  88.8 9.5 %collective-permute-start.8 = (bf16[384,128]{1,0:T(8,128)(2,1)S(1)}, bf16[384,128]{1,0:T(8,128)(2,1)S(1)}, u32[]{:S(2)}, u32[]{:S(2)}) collective-permute-start(bf16[384,128]{1,0:T(8,128)(2,1)S(1)} %fusion.75), channel_id=1, source_target_pairs={{1,0},{2,1},{3,2},{4,3},{5,4},{6,5},{7,6},{8,7},{9,8},{10,9},{11,1... | collective-permute-start | bytes 294920 | tf_op jit(solution)/shard_map/ppermute | solution.py:12
where the time goes:
time: 100 us; the launch traced here: 99.8 us
  starting transfers between devices  59.3 us (59%)
  matrix products  30.2 us (30%)
  local copies, waits for them, and re-layouts  4.12 us (4%)
  waiting for transfers between devices  3.04 us (3%)
  other arithmetic  1.95 us (2%)
  between operations  1.14 us (1%)
    ppermute x16, starting transfers between devices, from_behind(): return lax.ppermute(array, axis, pairs)  59.3 us
    dot_general x5, matrix products, block_grads(): jnp.einsum('hqk,qhd->kd', probs_half, grad_heads, preferred_element_type=...  8.65 us
    dot_general x5, matrix products, block_grads(): jnp.einsum('qhd,kd->hqk', grad_heads, value_block, preferred_element_type...  8.52 us
    dot_general x5, matrix products, block_grads(): jnp.einsum('qhd,kd->hqk', query_heads, key_block, preferred_element_type=...  5.09 us
    dot_general x5, matrix products, block_grads(): jnp.einsum('hqk,qhd->kd', dscores_half, query_heads, preferred_element_ty...  4.56 us
    dot_general x5, matrix products, block_grads(): jnp.einsum('hqk,kd->qhd', dscores_half, key_block, preferred_element_type...  3.42 us
    unnamed x19, local copies, waits for them, and re-layouts  3.24 us
    ppermute x16, waiting for transfers between devices, from_behind(): return lax.ppermute(array, axis, pairs)  3.04 us
  transfers between devices with their start and end apart: 16, of which 1 were waited for; matrix products, arithmetic and copies ran while one was open for 33% of the time, Pallas kernels for 0%

commit v1 on v0

v1 whole, which is shorter than its diff:
```python
import functools

import jax
import jax.numpy as jnp
from jax import lax
from jax.experimental import pallas as pl
from jax.experimental.pallas import tpu as pltpu
from jax.sharding import PartitionSpec as P

AXES = ("seq", "rep")
REACH = 4
HEADS = 8
HD = 128
TOK = 384
SCALE = HD**-0.5
LOG2E = 1.4426950408889634
FAR = 1e30

NT = (((1,), (1,)), ((), ()))
NN = (((1,), (0,)), ((), ()))
VM = pl.BlockSpec(memory_space=pltpu.VMEM)
SM = pl.BlockSpec(memory_space=pltpu.SMEM)


def dot(a, b, dims):
    return lax.dot_general(a, b, dims, preferred_element_type=jnp.float32)


def shift(array, by):
    length = lax.axis_size(AXES)
    pairs = [(i, i + by) for i in range(length) if 0 <= i + by < length]
    return lax.ppermute(array, AXES, pairs)


def prep_kernel(first_ref, lengths_ref, starts_ref):
    count = lengths_ref.shape[1]
    row = lax.broadcasted_iota(jnp.int32, (count, count), 0)
    col = lax.broadcasted_iota(jnp.int32, (count, count), 1)
    ends = jnp.sum(jnp.where(col <= row, lengths_ref[...], 0), axis=1, keepdims=True)
    first = first_ref[0]
    pos = first + lax.broadcasted_iota(jnp.int32, (1, TOK), 1)
    starts_ref[...] = jnp.max(jnp.where(ends <= pos, ends, 0), axis=0, keepdims=True) - first


def cross_kernel(distance, q, g, lse, delta, starts, kv, dq_in, dq, dkv, ps, dss):
    begin = starts[...]
    shared = begin <= 0
    key0 = jnp.max(jnp.where(lax.broadcasted_iota(jnp.int32, (1, TOK), 1) == 0, begin, -(2**30))) + TOK * distance

    def part(low):
        rows = TOK - low
        at = lax.broadcasted_iota(jnp.int32, (rows, 1), 0) + low
        live = at >= key0
        key = jnp.where(live, kv[low:, :HD], 0)
        value = jnp.where(live, kv[low:, HD:], 0)
        key_t = key.T
        for h in range(HEADS):
            hd = slice(h * HD, (h + 1) * HD)
            ht = slice(h * TOK, (h + 1) * TOK)
            l2 = jnp.where(shared, lse[h : h + 1, :] * LOG2E, FAR)
            s = dot(key, q[:, hd], NT)
            p = jnp.exp2(s * (SCALE * LOG2E) - l2)
            ds = p * (dot(value, g[:, hd], NT) - delta[h : h + 1, :])
            ps[low:, ht] = p.astype(jnp.bfloat16)
            dss[low:, ht] = ds.astype(jnp.bfloat16)
        for h in range(HEADS):
            ht = slice(h * TOK, (h + 1) * TOK)
            dq[h] = dq_in[h] + dot(key_t, dss[low:, ht], NN)
        dk = dv = None
        for h in range(HEADS):
            hd = slice(h * HD, (h + 1) * HD)
            ht = slice(h * TOK, (h + 1) * TOK)
            a = dot(ps[low:, ht], g[:, hd], NN)
            b = dot(dss[low:, ht], q[:, hd], NN)
            dv = a if dv is None else dv + a
            dk = b if dk is None else dk + b
        if low:
            dkv[:low, :] = jnp.zeros((low, 2 * HD), dkv.dtype)
        dkv[low:, :HD] = jnp.where(live, dk * SCALE, 0.0).astype(dkv.dtype)
        dkv[low:, HD:] = jnp.where(live, dv, 0.0).astype(dkv.dtype)

    @pl.when(key0 >= TOK)
    def _():
        dkv[...] = jnp.zeros_like(dkv)
        dq[...] = dq_in[...]

    @pl.when((key0 < TOK) & (key0 >= TOK - 128))
    def _():
        part(TOK - 128)

    @pl.when(key0 < TOK - 128)
    def _():
        part(0)


def own_kernel(q, g, lse, delta, starts, kv, dq, dkv, bias, ps, dss):
    begin = starts[...]
    at = lax.broadcasted_iota(jnp.int32, (TOK, TOK), 0)
    to = lax.broadcasted_iota(jnp.int32, (TOK, TOK), 1)
    bias[...] = jnp.where((at <= to) & (at >= begin), 0.0, -FAR)
    for j in range(0, TOK, 128):
        key = kv[j : j + 128, :HD]
        value = kv[j : j + 128, HD:]
        key_t = key.T
        for h in range(HEADS):
            hd = slice(h * HD, (h + 1) * HD)
            ht = slice(h * TOK + j, (h + 1) * TOK)
            s = dot(key, q[j:, hd], NT)
            p = jnp.exp2(s * (SCALE * LOG2E) - lse[h : h + 1, j:] * LOG2E + bias[j : j + 128, j:])
            ds = p * (dot(value, g[j:, hd], NT) - delta[h : h + 1, j:])
            ps[j : j + 128, ht] = p.astype(jnp.bfloat16)
            dss[j : j + 128, ht] = ds.astype(jnp.bfloat16)
    for j in range(0, TOK, 128):
        key_t = kv[: j + 128, :HD].T
        for h in range(HEADS):
            ht = slice(h * TOK + j, h * TOK + j + 128)
            dq[h, :, j : j + 128] = dot(key_t, dss[: j + 128, ht], NN)
    for j in range(0, TOK, 128):
        dk = dv = None
        for h in range(HEADS):
            hd = slice(h * HD, (h + 1) * HD)
            ht = slice(h * TOK + j, (h + 1) * TOK)
            a = dot(ps[j : j + 128, ht], g[j:, hd], NN)
            b = dot(dss[j : j + 128, ht], q[j:, hd], NN)
            dv = a if dv is None else dv + a
            dk = b if dk is None else dk + b
        dkv[j : j + 128, :HD] = dk * SCALE
        dkv[j : j + 128, HD:] = dv


def finish_kernel(dq, own, b1, b2, b3, b4, dq_out, dk_out, dv_out):
    for h in range(HEADS):
        dq_out[:, h * HD : (h + 1) * HD] = (dq[h] * SCALE).T.astype(dq_out.dtype)
    total = own[...]
    for b in (b1, b2, b3, b4):
        total = total + b[...].astype(jnp.float32)
    dk_out[...] = total[:, :HD].astype(dk_out.dtype)
    dv_out[...] = total[:, HD:].astype(dv_out.dtype)


def params(**more):
    return pltpu.CompilerParams(vmem_limit_bytes=24 << 20, **more)


def cost(flops):
    return pl.CostEstimate(flops=flops, bytes_accessed=4 << 20, transcendentals=0)


PAIR = 10 * HEADS * TOK * TOK * HD


def shards(query_rows, key_rows, value_rows, out_grad, logsumexp, row_delta, doc_lengths):
    bf, f32 = jnp.bfloat16, jnp.float32
    first = (lax.axis_index(AXES) * TOK).astype(jnp.int32).reshape(1)
    kv = jnp.concatenate([key_rows, value_rows], 1)
    arrived = {d: shift(kv, d) for d in (1, 2, 3, 4)}
    starts = pl.pallas_call(
        prep_kernel,
        out_shape=jax.ShapeDtypeStruct((1, TOK), jnp.int32),
        in_specs=[SM, VM],
        out_specs=VM,
        compiler_params=params(),
        name="prep",
    )(first, doc_lengths.reshape(1, -1))
    dq_shape = jax.ShapeDtypeStruct((HEADS, HD, TOK), f32)
    half = pltpu.VMEM((TOK, HEADS * TOK), bf)
    dq, own = pl.pallas_call(
        own_kernel,
        out_shape=[dq_shape, jax.ShapeDtypeStruct((TOK, 2 * HD), f32)],
        in_specs=[VM] * 6,
        out_specs=[VM] * 2,
        scratch_shapes=[pltpu.VMEM((TOK, TOK), f32), half, half],
        compiler_params=params(),
        cost_estimate=cost(PAIR),
        name="own",
    )(query_rows, out_grad, logsumexp, row_delta, starts, kv)
    returned = {}
    for d in (1, 2, 3, 4):
        dq, part = pl.pallas_call(
            functools.partial(cross_kernel, d),
            out_shape=[dq_shape, jax.ShapeDtypeStruct((TOK, 2 * HD), bf)],
            in_specs=[VM] * 7,
            out_specs=[VM] * 2,
            scratch_shapes=[half, half],
            input_output_aliases={6: 0},
            compiler_params=params(),
            cost_estimate=cost(PAIR),
            name=f"cross{d}",
        )(query_rows, out_grad, logsumexp, row_delta, starts, arrived[d], dq)
        returned[d] = shift(part, -d)
    return pl.pallas_call(
        finish_kernel,
        out_shape=[
            jax.ShapeDtypeStruct((TOK, HEADS * HD), bf),
            jax.ShapeDtypeStruct((TOK, HD), bf),
            jax.ShapeDtypeStruct((TOK, HD), bf),
        ],
        in_specs=[VM] * 6,
        out_specs=[VM] * 3,
        compiler_params=params(),
        name="finish",
    )(dq, own, *[returned[d] for d in (1, 2, 3, 4)])


def solution(mesh):
    rows = P(AXES, None)
    return jax.shard_map(
        shards,
        mesh=mesh,
        in_specs=(rows, rows, rows, rows, P(None, AXES), P(None, AXES), P()),
        out_specs=(rows, rows, rows),
        check_vma=False,
    )
```

time: 100 us -> 57.6 us (0.58)
  the two profiles are of different devices: /device:TPU:145 before, /device:TPU:127 now
where the time goes in v1:
time: 57.6 us; the launch traced here: 57.4 us
  starting transfers between devices  32.1 us (56%)
  waiting for transfers between devices  10.4 us (18%)
  Pallas kernels  7.87 us (14%)
  local copies, waits for them, and re-layouts  6.18 us (11%)
  between operations  0.82 us (1%)
    ppermute x8, starting transfers between devices, shift(): return lax.ppermute(array, AXES, pairs)  32.1 us
    ppermute x8, waiting for transfers between devices, shift(): return lax.ppermute(array, AXES, pairs)  10.4 us
    unnamed x11, local copies, waits for them, and re-layouts  5.26 us
    pallas_call x4, Pallas kernels, shards(): pl.pallas_call(functools.partial(cross_kernel, d), out_shape=[dq_shape, j...  3.55 us
    pallas_call x1, Pallas kernels, shards(): pl.pallas_call(own_kernel, out_shape=[dq_shape, jax.ShapeDtypeStruct((TOK...  2.92 us
    pallas_call x1, Pallas kernels, shards(): pl.pallas_call(finish_kernel, out_shape=[jax.ShapeDtypeStruct((TOK, HEADS...  1.23 us
  transfers between devices with their start and end apart: 8, of which 2 were waited for; matrix products, arithmetic and copies ran while one was open for 0% of the time, Pallas kernels for 10%

profile of v1, /device:TPU:127, one launch (start us, length us, event | category | flops | bytes accessed | tf_op | source)
XLA Modules:
  0.0 57.4 jit_solution(2973219124350667563)
XLA Ops:
  0.6 0.9 %constant_dynamic-update-slice_fusion.1 = bf16[384,256]{1,0:T(8,128)(2,1)S(1)} fusion(bf16[384,128]{1,0:T(8,128)(2,1)} %param.8), kind=kLoop, calls=%fused_computation.1 | loop fusion | bytes 196608
  1.5 0.9 %constant_dynamic-update-slice_fusion.kv = bf16[384,256]{1,0:T(8,128)(2,1)S(1)} fusion(bf16[384,256]{1,0:T(8,128)(2,1)S(1)} %constant_dynamic-update-slice_fusion.1, bf16[384,128]{1,0:T(8,128)(2,1)} %param.9), kind=kLoop, calls=%fused_computation | loop fusion | bytes 196608 | tf_op jit(solution)/shard_map/concatenate | solution.py:155
  2.5 4.9 %collective-permute-start.3 = (bf16[384,256]{1,0:T(8,128)(2,1)S(1)}, bf16[384,256]{1,0:T(8,128)(2,1)S(1)}, u32[]{:S(2)}, u32[]{:S(2)}) collective-permute-start(bf16[384,256]{1,0:T(8,128)(2,1)S(1)} %constant_dynamic-update-slice_fusion.kv), channel_id=1, source_target_pairs={{0,1},{1,2},{2,3},{3,4},{4,5},{5,6},{6,7},{7,8},{8,9},{9,10},{10,1... | collective-permute-start | bytes 589832 | tf_op jit(solution)/shard_map/ppermute | solution.py:32
  7.4 4.3 %collective-permute-start.2 = (bf16[384,256]{1,0:T(8,128)(2,1)S(1)}, bf16[384,256]{1,0:T(8,128)(2,1)S(1)}, u32[]{:S(2)}, u32[]{:S(2)}) collective-permute-start(bf16[384,256]{1,0:T(8,128)(2,1)S(1)} %constant_dynamic-update-slice_fusion.kv), channel_id=1, source_target_pairs={{0,2},{1,3},{2,4},{3,5},{4,6},{5,7},{6,8},{7,9},{8,10},{9,11},{10,... | collective-permute-start | bytes 589832 | tf_op jit(solution)/shard_map/ppermute | solution.py:32
  11.7 1.9 %collective-permute-start.1 = (bf16[384,256]{1,0:T(8,128)(2,1)S(1)}, bf16[384,256]{1,0:T(8,128)(2,1)S(1)}, u32[]{:S(2)}, u32[]{:S(2)}) collective-permute-start(bf16[384,256]{1,0:T(8,128)(2,1)S(1)} %constant_dynamic-update-slice_fusion.kv), channel_id=1, source_target_pairs={{0,3},{1,4},{2,5},{3,6},{4,7},{5,8},{6,9},{7,10},{8,11},{9,12},{10... | collective-permute-start | bytes 589832 | tf_op jit(solution)/shard_map/ppermute | solution.py:32
  13.6 3.1 %collective-permute-start = (bf16[384,256]{1,0:T(8,128)(2,1)S(1)}, bf16[384,256]{1,0:T(8,128)(2,1)S(1)}, u32[]{:S(2)}, u32[]{:S(2)}) collective-permute-start(bf16[384,256]{1,0:T(8,128)(2,1)S(1)} %constant_dynamic-update-slice_fusion.kv), channel_id=1, source_target_pairs={{0,4},{1,5},{2,6},{3,7},{4,8},{5,9},{6,10},{7,11},{8,12},{9,13},{1... | collective-permute-start | bytes 589832 | tf_op jit(solution)/shard_map/ppermute | solution.py:32
  16.8 0.0 copy-start
  16.8 0.7 %copy-done = s32[255]{0:T(256)S(1)} copy-done((s32[255]{0:T(256)S(1)}, s32[255]{0:T(256)}, u32[]{:S(2)}) %copy-start) | copy-done | bytes 1044
  17.4 0.2 prep.1.starts
  17.6 0.0 copy-start.1
  17.6 1.1 %copy-done.1 = bf16[384,1024]{1,0:T(8,128)(2,1)S(1)} copy-done((bf16[384,1024]{1,0:T(8,128)(2,1)S(1)}, bf16[384,1024]{1,0:T(8,128)(2,1)}, u32[]{:S(2)}) %copy-start.1) | copy-done | bytes 786456
  18.8 1.1 %copy-done.2 = bf16[384,1024]{1,0:T(8,128)(2,1)S(1)} copy-done((bf16[384,1024]{1,0:T(8,128)(2,1)S(1)}, bf16[384,1024]{1,0:T(8,128)(2,1)}, u32[]{:S(2)}) %copy-start.2) | copy-done | bytes 786456
  19.9 0.7 %copy-done.3 = f32[8,384]{1,0:T(8,128)S(1)} copy-done((f32[8,384]{1,0:T(8,128)S(1)}, f32[8,384]{1,0:T(8,128)}, u32[]{:S(2)}) %copy-start.3) | copy-done | bytes 12312
  20.6 0.7 %copy-done.4 = f32[8,384]{1,0:T(8,128)S(1)} copy-done((f32[8,384]{1,0:T(8,128)S(1)}, f32[8,384]{1,0:T(8,128)}, u32[]{:S(2)}) %copy-start.4) | copy-done | bytes 12312
  21.3 2.9 %own.1 = (f32[8,128,384]{2,1,0:T(8,128)S(1)}, f32[384,256]{1,0:T(8,128)S(1)}) custom-call(bf16[384,1024]{1,0:T(8,128)(2,1)S(1)} %copy-done.1, bf16[384,1024]{1,0:T(8,128)(2,1)S(1)} %copy-done.2, f32[8,384]{1,0:T(8,128)S(1)} %copy-done.3, f32[8,384]{1,0:T(8,128)S(1)} %copy-done.4, s32[1,384]{1,0:T(1,128)S(1)} %prep.1.starts, ...), custom_call_target="tpu_custom_call" | custom-call | flops 1509949440 | bytes 4194304 | tf_op jit(solution)/shard_map/own/pallas_call | solution.py:167
  24.2 0.0 collective-permute-done.3.kv
  24.2 1.9 %cross1.1 = (f32[8,128,384]{2,1,0:T(8,128)S(1)}, bf16[384,256]{1,0:T(8,128)(2,1)S(1)}) custom-call(bf16[384,1024]{1,0:T(8,128)(2,1)S(1)} %copy-done.1, bf16[384,1024]{1,0:T(8,128)(2,1)S(1)} %copy-done.2, f32[8,384]{1,0:T(8,128)S(1)} %copy-done.3, f32[8,384]{1,0:T(8,128)S(1)} %copy-done.4, s32[1,384]{1,0:T(1,128)S(1)} %prep.1.starts, ...), custom_call_target="tpu_custom_call", output_to_operand_aliasing={{0}: (6, {})} | custom-call | flops 1509949440 | bytes 4194304 | tf_op jit(solution)/shard_map/cross1/pallas_call | solution.py:179
  26.1 0.0 collective-permute-done.2.kv
  26.1 0.6 %cross2.1 = (f32[8,128,384]{2,1,0:T(8,128)S(1)}, bf16[384,256]{1,0:T(8,128)(2,1)S(1)}) custom-call(bf16[384,1024]{1,0:T(8,128)(2,1)S(1)} %copy-done.1, bf16[384,1024]{1,0:T(8,128)(2,1)S(1)} %copy-done.2, f32[8,384]{1,0:T(8,128)S(1)} %copy-done.3, f32[8,384]{1,0:T(8,128)S(1)} %copy-done.4, s32[1,384]{1,0:T(1,128)S(1)} %prep.1.starts, ...), custom_call_target="tpu_custom_call", output_to_operand_aliasing={{0}: (6, {})} | custom-call | flops 1509949440 | bytes 4194304 | tf_op jit(solution)/shard_map/cross2/pallas_call | solution.py:179
  26.7 0.0 collective-permute-done.1.kv
  26.8 0.4 cross3.1
  27.2 0.0 collective-permute-done.kv
  27.2 0.6 %cross4.1 = (f32[8,128,384]{2,1,0:T(8,128)S(1)}, bf16[384,256]{1,0:T(8,128)(2,1)S(1)}) custom-call(bf16[384,1024]{1,0:T(8,128)(2,1)S(1)} %copy-done.1, bf16[384,1024]{1,0:T(8,128)(2,1)S(1)} %copy-done.2, f32[8,384]{1,0:T(8,128)S(1)} %copy-done.3, f32[8,384]{1,0:T(8,128)S(1)} %copy-done.4, s32[1,384]{1,0:T(1,128)S(1)} %prep.1.starts, ...), custom_call_target="tpu_custom_call", output_to_operand_aliasing={{0}: (6, {})} | custom-call | flops 1509949440 | bytes 4194304 | tf_op jit(solution)/shard_map/cross4/pallas_call | solution.py:179
  27.9 6.3 %collective-permute-start.7 = (bf16[384,256]{1,0:T(8,128)(2,1)S(1)}, bf16[384,256]{1,0:T(8,128)(2,1)S(1)}, u32[]{:S(2)}, u32[]{:S(2)}) collective-permute-start(bf16[384,256]{1,0:T(8,128)(2,1)S(1)} %get-tuple-element.22), channel_id=1, source_target_pairs={{4,0},{5,1},{6,2},{7,3},{8,4},{9,5},{10,6},{11,7},{12,8},{13,9},{1... | collective-permute-start | bytes 589832 | tf_op jit(solution)/shard_map/ppermute | solution.py:32
  34.1 1.9 %collective-permute-start.6 = (bf16[384,256]{1,0:T(8,128)(2,1)S(1)}, bf16[384,256]{1,0:T(8,128)(2,1)S(1)}, u32[]{:S(2)}, u32[]{:S(2)}) collective-permute-start(bf16[384,256]{1,0:T(8,128)(2,1)S(1)} %get-tuple-element.21), channel_id=1, source_target_pairs={{3,0},{4,1},{5,2},{6,3},{7,4},{8,5},{9,6},{10,7},{11,8},{12,9},{13... | collective-permute-start | bytes 589832 | tf_op jit(solution)/shard_map/ppermute | solution.py:32
  36.0 5.4 %collective-permute-start.5 = (bf16[384,256]{1,0:T(8,128)(2,1)S(1)}, bf16[384,256]{1,0:T(8,128)(2,1)S(1)}, u32[]{:S(2)}, u32[]{:S(2)}) collective-permute-start(bf16[384,256]{1,0:T(8,128)(2,1)S(1)} %get-tuple-element.20), channel_id=1, source_target_pairs={{2,0},{3,1},{4,2},{5,3},{6,4},{7,5},{8,6},{9,7},{10,8},{11,9},{12,... | collective-permute-start | bytes 589832 | tf_op jit(solution)/shard_map/ppermute | solution.py:32
  41.5 4.3 %collective-permute-start.4 = (bf16[384,256]{1,0:T(8,128)(2,1)S(1)}, bf16[384,256]{1,0:T(8,128)(2,1)S(1)}, u32[]{:S(2)}, u32[]{:S(2)}) collective-permute-start(bf16[384,256]{1,0:T(8,128)(2,1)S(1)} %get-tuple-element.19), channel_id=1, source_target_pairs={{1,0},{2,1},{3,2},{4,3},{5,4},{6,5},{7,6},{8,7},{9,8},{10,9},{11,1... | collective-permute-start | bytes 589832 | tf_op jit(solution)/shard_map/ppermute | solution.py:32
  45.7 0.0 collective-permute-done.7.b4
  45.8 0.0 collective-permute-done.6.b3
  45.8 3.5 %collective-permute-done.5.b2 = bf16[384,256]{1,0:T(8,128)(2,1)S(1)} collective-permute-done((bf16[384,256]{1,0:T(8,128)(2,1)S(1)}, bf16[384,256]{1,0:T(8,128)(2,1)S(1)}, u32[]{:S(2)}, u32[]{:S(2)}) %collective-permute-start.5) | collective-permute-done | bytes 196640 | tf_op jit(solution)/shard_map/ppermute | solution.py:32
  49.3 6.9 %collective-permute-done.4.b1 = bf16[384,256]{1,0:T(8,128)(2,1)S(1)} collective-permute-done((bf16[384,256]{1,0:T(8,128)(2,1)S(1)}, bf16[384,256]{1,0:T(8,128)(2,1)S(1)}, u32[]{:S(2)}, u32[]{:S(2)}) %collective-permute-start.4) | collective-permute-done | bytes 196640 | tf_op jit(solution)/shard_map/ppermute | solution.py:32
  56.1 1.2 %finish.1 = (bf16[384,1024]{1,0:T(8,128)(2,1)}, bf16[384,128]{1,0:T(8,128)(2,1)}, bf16[384,128]{1,0:T(8,128)(2,1)}) custom-call(f32[8,128,384]{2,1,0:T(8,128)S(1)} %get-tuple-element.17.dq, f32[384,256]{1,0:T(8,128)S(1)} %get-tuple-element.18.own, bf16[384,256]{1,0:T(8,128)(2,1)S(1)} %collective-permute-done.4.b1, ...), custom_call_target="tpu_custom_call" | custom-call | tf_op jit(solution)/shard_map/finish/pallas_call | solution.py:191
  (3 shorter events, 0.0 us)
Async XLA Ops:
  2.5 21.8 %collective-permute-start.3 = (bf16[384,256]{1,0:T(8,128)(2,1)S(1)}, bf16[384,256]{1,0:T(8,128)(2,1)S(1)}, u32[]{:S(2)}, u32[]{:S(2)}) collective-permute-start(bf16[384,256]{1,0:T(8,128)(2,1)S(1)} %constant_dynamic-update-slice_fusion.kv), channel_id=1, source_target_pairs={{0,1},{1,2},{2,3},{3,4},{4,5},{5,6},{6,7},{7,8},{8,9},{9,10},{10,1... | collective-permute-start | bytes 589832 | tf_op jit(solution)/shard_map/ppermute | solution.py:32
  7.4 18.8 %collective-permute-start.2 = (bf16[384,256]{1,0:T(8,128)(2,1)S(1)}, bf16[384,256]{1,0:T(8,128)(2,1)S(1)}, u32[]{:S(2)}, u32[]{:S(2)}) collective-permute-start(bf16[384,256]{1,0:T(8,128)(2,1)S(1)} %constant_dynamic-update-slice_fusion.kv), channel_id=1, source_target_pairs={{0,2},{1,3},{2,4},{3,5},{4,6},{5,7},{6,8},{7,9},{8,10},{9,11},{10,... | collective-permute-start | bytes 589832 | tf_op jit(solution)/shard_map/ppermute | solution.py:32
  11.7 15.0 %collective-permute-start.1 = (bf16[384,256]{1,0:T(8,128)(2,1)S(1)}, bf16[384,256]{1,0:T(8,128)(2,1)S(1)}, u32[]{:S(2)}, u32[]{:S(2)}) collective-permute-start(bf16[384,256]{1,0:T(8,128)(2,1)S(1)} %constant_dynamic-update-slice_fusion.kv), channel_id=1, source_target_pairs={{0,3},{1,4},{2,5},{3,6},{4,7},{5,8},{6,9},{7,10},{8,11},{9,12},{10... | collective-permute-start | bytes 589832 | tf_op jit(solution)/shard_map/ppermute | solution.py:32
  13.6 13.6 %collective-permute-start = (bf16[384,256]{1,0:T(8,128)(2,1)S(1)}, bf16[384,256]{1,0:T(8,128)(2,1)S(1)}, u32[]{:S(2)}, u32[]{:S(2)}) collective-permute-start(bf16[384,256]{1,0:T(8,128)(2,1)S(1)} %constant_dynamic-update-slice_fusion.kv), channel_id=1, source_target_pairs={{0,4},{1,5},{2,6},{3,7},{4,8},{5,9},{6,10},{7,11},{8,12},{9,13},{1... | collective-permute-start | bytes 589832 | tf_op jit(solution)/shard_map/ppermute | solution.py:32
  16.8 0.7 %copy-start = (s32[255]{0:T(256)S(1)}, s32[255]{0:T(256)}, u32[]{:S(2)}) copy-start(s32[255]{0:T(256)} %param.13) | copy-start | bytes 3064
  17.6 1.1 %copy-start.1 = (bf16[384,1024]{1,0:T(8,128)(2,1)S(1)}, bf16[384,1024]{1,0:T(8,128)(2,1)}, u32[]{:S(2)}) copy-start(bf16[384,1024]{1,0:T(8,128)(2,1)} %q.9) | copy-start | bytes 2359300
  18.8 1.1 %copy-start.2 = (bf16[384,1024]{1,0:T(8,128)(2,1)S(1)}, bf16[384,1024]{1,0:T(8,128)(2,1)}, u32[]{:S(2)}) copy-start(bf16[384,1024]{1,0:T(8,128)(2,1)} %g.9) | copy-start | bytes 2359300
  19.9 0.7 %copy-start.3 = (f32[8,384]{1,0:T(8,128)S(1)}, f32[8,384]{1,0:T(8,128)}, u32[]{:S(2)}) copy-start(f32[8,384]{1,0:T(8,128)} %lse.9) | copy-start | bytes 36868
  20.6 0.7 %copy-start.4 = (f32[8,384]{1,0:T(8,128)S(1)}, f32[8,384]{1,0:T(8,128)}, u32[]{:S(2)}) copy-start(f32[8,384]{1,0:T(8,128)} %delta.9) | copy-start | bytes 36868
  27.9 17.9 %collective-permute-start.7 = (bf16[384,256]{1,0:T(8,128)(2,1)S(1)}, bf16[384,256]{1,0:T(8,128)(2,1)S(1)}, u32[]{:S(2)}, u32[]{:S(2)}) collective-permute-start(bf16[384,256]{1,0:T(8,128)(2,1)S(1)} %get-tuple-element.22), channel_id=1, source_target_pairs={{4,0},{5,1},{6,2},{7,3},{8,4},{9,5},{10,6},{11,7},{12,8},{13,9},{1... | collective-permute-start | bytes 589832 | tf_op jit(solution)/shard_map/ppermute | solution.py:32
  34.1 11.6 %collective-permute-start.6 = (bf16[384,256]{1,0:T(8,128)(2,1)S(1)}, bf16[384,256]{1,0:T(8,128)(2,1)S(1)}, u32[]{:S(2)}, u32[]{:S(2)}) collective-permute-start(bf16[384,256]{1,0:T(8,128)(2,1)S(1)} %get-tuple-element.21), channel_id=1, source_target_pairs={{3,0},{4,1},{5,2},{6,3},{7,4},{8,5},{9,6},{10,7},{11,8},{12,9},{13... | collective-permute-start | bytes 589832 | tf_op jit(solution)/shard_map/ppermute | solution.py:32
  36.0 13.2 %collective-permute-start.5 = (bf16[384,256]{1,0:T(8,128)(2,1)S(1)}, bf16[384,256]{1,0:T(8,128)(2,1)S(1)}, u32[]{:S(2)}, u32[]{:S(2)}) collective-permute-start(bf16[384,256]{1,0:T(8,128)(2,1)S(1)} %get-tuple-element.20), channel_id=1, source_target_pairs={{2,0},{3,1},{4,2},{5,3},{6,4},{7,5},{8,6},{9,7},{10,8},{11,9},{12,... | collective-permute-start | bytes 589832 | tf_op jit(solution)/shard_map/ppermute | solution.py:32
  41.5 14.7 %collective-permute-start.4 = (bf16[384,256]{1,0:T(8,128)(2,1)S(1)}, bf16[384,256]{1,0:T(8,128)(2,1)S(1)}, u32[]{:S(2)}, u32[]{:S(2)}) collective-permute-start(bf16[384,256]{1,0:T(8,128)(2,1)S(1)} %get-tuple-element.19), channel_id=1, source_target_pairs={{1,0},{2,1},{3,2},{4,3},{5,4},{6,5},{7,6},{8,7},{9,8},{10,9},{11,1... | collective-permute-start | bytes 589832 | tf_op jit(solution)/shard_map/ppermute | solution.py:32
